TPU v7x, 128 devices: a whole 4x4x4 slice. The times are simulated.
128 devices in a mesh: row: 8 (over z, core), col: 16 (over x, y).
Axes of the slice: x: 4, y: 4, z: 4, core: 2. Of those that a mesh axis runs over, the one named last changes fastest.
Arguments:
- factor_panel: bfloat16 [4096, 31, 16, 256], P('row', None, 'col'), may hold values from -0.015625 to 0.015625
- solved_prev: bfloat16 [31, 16, 256, 512], P(None, 'col'), may hold values from -6 to 6
- rhs_last: float32 [4096, 512], P('row', 'col'), may hold values from -6 to 6
- inv_last: bfloat16 [4096, 4096], P('row'), may hold values from -1 to 3, as said below
- inv_prev: bfloat16 [1, 16, 256, 4096], P(None, 'col'), may hold values from -1 to 3, as said below
Outputs:
- updated_rhs: float32 [512, 31, 16, 256], P('row', None, 'col')
- solution_last: float32 [4096, 512], P('row', 'col')
- solution_prev: float32 [4096, 512], P('col', 'row')
Inputs may be any that keep to these rules, and one draw needn't show every extreme that they name: `inv_last`: lower triangular with a positive diagonal. `inv_prev`: as a 4096 x 4096 matrix, lower triangular with a positive diagonal.
All inputs are finite; a program needn't handle non-finite values.
Results may differ from a plain program's by a relative error of at most 0.0055.
Values may be sent and summed in bfloat16 or wider, within the bound.
A program may use at most 128 MiB of HBM per device.

v0:
```python
import jax
import jax.numpy as jnp
from jax import lax
from jax.sharding import PartitionSpec as P


def transposed_terms(matrix, operand):
    return lax.dot_general(
        matrix, operand, (((0,), (0,)), ((), ())), preferred_element_type=jnp.float32
    )


def previous_solution(prior_values, inv_prev):
    prior_block = prior_values.astype(jnp.bfloat16)
    inverse_rows = inv_prev.reshape(inv_prev.shape[0] * inv_prev.shape[2], inv_prev.shape[3])
    return lax.psum_scatter(
        lax.dot_general(
            inverse_rows, prior_block, (((0,), (1,)), ((), ())), preferred_element_type=jnp.float32
        ),
        "col",
        scatter_dimension=0,
        tiled=True,
    )


def update_terms(solution_half, factor):
    return lax.dot_general(
        solution_half, factor, (((0,), (0,)), ((), ())), preferred_element_type=jnp.float32
    )


def per_device(factor_panel, solved_prev, rhs_last, inv_last, inv_prev):
    row_share = factor_panel.shape[0]
    rounds = factor_panel.shape[1]
    block_cols = factor_panel.shape[3]
    side_count = solved_prev.shape[3]
    factor = factor_panel.reshape(row_share, rounds * block_cols)
    known = solved_prev.reshape(rounds * block_cols, side_count)
    partial_value = jnp.dot(factor, known, preferred_element_type=jnp.float32)
    own_share = lax.psum_scatter(partial_value, "col", scatter_dimension=1, tiled=True)
    residue = (rhs_last - own_share).astype(jnp.bfloat16)
    stacked = lax.all_gather(residue, "row", axis=0, tiled=True)
    forward_last = jnp.dot(inv_last, stacked, preferred_element_type=jnp.float32).astype(
        jnp.bfloat16
    )
    solution_last = lax.psum_scatter(
        transposed_terms(inv_last, forward_last), "row", scatter_dimension=0, tiled=True
    )
    solution_half = lax.all_gather(solution_last.astype(jnp.bfloat16), "col", axis=1, tiled=True)
    out_share = side_count // lax.axis_size("row")
    keep_rounds = inv_prev.shape[0]
    split_at = (rounds - keep_rounds) * block_cols
    offset = lax.axis_index("row") * out_share
    start_values = lax.dynamic_slice_in_dim(known, offset, out_share, 1).T.astype(jnp.float32)
    all_terms = lax.psum_scatter(
        update_terms(solution_half, factor), "row", scatter_dimension=0, tiled=True
    )
    updated = start_values - all_terms
    solution_prev = previous_solution(updated[:, split_at:], inv_prev)
    updated_rhs = updated.reshape(out_share, rounds, 1, block_cols)
    return (updated_rhs, solution_last, solution_prev)


def solution(mesh):
    in_specs = (
        P("row", None, "col", None),
        P(None, "col", None, None),
        P("row", "col"),
        P("row", None),
        P(None, "col", None, None),
    )
    out_specs = (P("row", None, "col", None), P("row", "col"), P("col", "row"))
    return jax.shard_map(
        per_device, mesh=mesh, in_specs=in_specs, out_specs=out_specs, check_vma=False
    )
```

profile of v0, /device:TPU:0, one launch (start us, length us, event | category | flops | bytes accessed | tf_op | source)
XLA Modules:
  0.0 350.4 jit_solution(9653179033184075488)
XLA Ops:
  7.2 0.0 copy-start
  7.2 0.0 copy-start.2
  7.2 0.0 reduce-scatter.5.cloned.1.call-start
  7.2 11.1 %fusion.4 = f32[512,512]{0,1:T(8,128)} fusion(bf16[31,1,256,512]{3,2,1,0:T(8,128)(2,1)} %param.6, bf16[512,31,1,256]{3,0,2,1:T(8,128)(2,1)} %param.5), kind=kOutput, calls=%fused_computation.7 | convolution fusion | flops 4160749568 | bytes 17301504 | tf_op jit(solution)/shard_map/dot_general | solution.py:39
  18.4 0.0 reduce-scatter.5.cloned.1.call-update
  18.4 0.0 reduce-scatter.7.cloned.1.call-start
  18.4 75.3 %reduce-scatter.5.cloned.1.call-done = f32[512,32]{0,1:T(8,128)} async-done(((f32[512,512]{0,1:T(8,128)}), f32[512,32]{0,1:T(8,128)}) %reduce-scatter.5.cloned.1.call-update) | async-done | bytes 65552 | tf_op jit(solution)/shard_map/reduce_scatter | solution.py:40
  93.8 0.0 copy-done.2
  93.8 0.9 subtract_convert_fusion
  94.6 13.3 %all_gather.6 = bf16[4096,32]{0,1:T(8,128)(2,1)S(1)} all-gather(bf16[512,32]{0,1:T(8,128)(2,1)S(1)} %subtract_convert_fusion), channel_id=1, replica_groups=mesh['row'=8,'col'=16] {'row'}, dimensions={0}, use_global_device_ids=true | all-gather | bytes 294912 | tf_op jit(solution)/shard_map/all_gather | solution.py:42
  108.0 6.4 %convolution_bitcast_fusion.1 = f32[4096,32]{0,1:T(8,128)} fusion(bf16[512,4096]{1,0:T(8,128)(2,1)} %param.8, bf16[4096,32]{0,1:T(8,128)(2,1)S(1)} %all_gather.6), kind=kOutput, calls=%fused_computation.4 | convolution fusion | flops 268451840 | bytes 4980736 | tf_op jit(solution)/shard_map/dot_general | solution.py:8
  114.4 0.0 reduce-scatter.7.cloned.1.call-update
  114.4 0.0 reduce-scatter.9.cloned.1.call-start
  114.5 11.5 %copy.11 = bf16[512,31,1,256]{0,3,1,2:T(8,128)(2,1)} copy(bf16[512,31,1,256]{3,0,2,1:T(8,128)(2,1)} %param.5) | data formatting | bytes 16252928 | tf_op args[0]
  126.0 18.4 %reduce-scatter.7.cloned.1.call-done = f32[512,32]{0,1:T(8,128)} async-done(((f32[4096,32]{0,1:T(8,128)}), f32[512,32]{0,1:T(8,128)}) %reduce-scatter.7.cloned.1.call-update) | async-done | bytes 65552 | tf_op jit(solution)/shard_map/reduce_scatter | solution.py:46
  144.4 0.8 convert_element_type.21
  145.2 24.0 %all_gather.7 = bf16[512,512]{0,1:T(8,128)(2,1)S(1)} all-gather(bf16[512,32]{0,1:T(8,128)(2,1)S(1)} %convert_element_type.21), channel_id=1, replica_groups=mesh['row'=8,'col'=16] {'col'}, dimensions={1}, use_global_device_ids=true | all-gather | bytes 557056 | tf_op jit(solution)/shard_map/all_gather | solution.py:49
  169.2 11.2 %fusion.9 = f32[512,7936]{1,0:T(8,128)} fusion(bf16[512,512]{0,1:T(8,128)(2,1)S(1)} %all_gather.7, bf16[512,7936]{0,1:T(8,128)(2,1)} %bitcast.28), kind=kOutput, calls=%fused_computation.12 | convolution fusion | flops 4160749568 | bytes 24903680 | tf_op jit(solution)/shard_map/dot_general | solution.py:27
  180.5 0.0 reduce-scatter.9.cloned.1.call-update
  180.5 0.2 reduce-scatter.11.cloned.1.call-start
  180.7 3.5 constant_dynamic-slice_fusion
  184.2 2.0 copy.13
  186.2 80.7 %reduce-scatter.9.cloned.1.call-done = f32[64,7936]{1,0:T(8,128)} async-done(((f32[512,7936]{1,0:T(8,128)}), f32[64,7936]{1,0:T(8,128)}) %reduce-scatter.9.cloned.1.call-update) | async-done | bytes 2031632 | tf_op jit(solution)/shard_map/reduce_scatter | solution.py:55
  266.9 1.7 bitcast_subtract_fusion
  268.7 0.0 copy-start.1
  268.7 1.3 copy-done.1
  270.0 0.0 copy-done
  270.0 1.5 convolution_bitcast_fusion
  271.5 0.0 reduce-scatter.11.cloned.1.call-update
  271.5 4.3 %reshape.31 = f32[64,31,1,256]{3,2,1,0:T(1,128)} reshape(f32[64,7936]{1,0:T(8,128)} %copy-done.1) | data formatting | bytes 4063232 | tf_op jit(solution)/shard_map/reshape | solution.py:60
  275.8 68.1 %reduce-scatter.11.cloned.1.call-done = f32[256,64]{0,1:T(8,128)} async-done(((f32[4096,64]{0,1:T(8,128)}), f32[256,64]{0,1:T(8,128)}) %reduce-scatter.11.cloned.1.call-update) | async-done | bytes 65552 | tf_op jit(solution)/shard_map/reduce_scatter | solution.py:16
Async XLA Ops:
  7.2 262.8 %copy-start = (bf16[1,1,256,4096]{3,2,1,0:T(8,128)(2,1)S(1)}, bf16[1,1,256,4096]{3,2,1,0:T(8,128)(2,1)}, u32[]{:S(2)}) copy-start(bf16[1,1,256,4096]{3,2,1,0:T(8,128)(2,1)} %param.9) | copy-start | bytes 6291460
  7.2 86.6 %copy-start.2 = (f32[512,32]{0,1:T(8,128)S(1)}, f32[512,32]{0,1:T(8,128)}, u32[]{:S(2)}) copy-start(f32[512,32]{0,1:T(8,128)} %param.7) | copy-start | bytes 196612
  7.2 86.6 %reduce-scatter.5.cloned.1.call-start = ((), (), s32[]{:S(2)}) async-start(), calls=%async_computation.4 | async-start | bytes 1114112 | tf_op jit(solution)/shard_map/reduce_scatter | solution.py:40
  18.4 126.0 %reduce-scatter.7.cloned.1.call-start = ((), (), s32[]{:S(2)}) async-start(), calls=%async_computation.5 | async-start | bytes 589824 | tf_op jit(solution)/shard_map/reduce_scatter | solution.py:46
  114.4 152.5 %reduce-scatter.9.cloned.1.call-start = ((), (), s32[]{:S(2)}) async-start(), calls=%async_computation.6 | async-start | bytes 18284544 | tf_op jit(solution)/shard_map/reduce_scatter | solution.py:55
  180.5 163.4 %reduce-scatter.11.cloned.1.call-start = ((), (), s32[]{:S(2)}) async-start(), calls=%async_computation.7 | async-start | bytes 1114112 | tf_op jit(solution)/shard_map/reduce_scatter | solution.py:16
  268.7 1.3 copy-start.1
Sparse Core Ops, SparseCore 0:
  18.5 75.2 reduce-scatter.4
  114.5 29.7 reduce-scatter.6
  180.6 86.2 reduce-scatter.8
  271.6 72.2 reduce-scatter.10
where the time goes:
time: 351 us; the launch traced here: 350 us
  waiting for transfers between devices  243 us (69%)
  blocking collectives  37.3 us (11%)
  matrix products  30.2 us (9%)
  local copies, waits for them, and re-layouts  22.6 us (6%)
  between operations  13.8 us (4%)
    reduce_scatter x1, waiting for transfers between devices, per_device(): lax.psum_scatter(update_terms(solution_half, factor), 'row', scatter_dime...  80.7 us
    reduce_scatter x1, waiting for transfers between devices, per_device(): lax.psum_scatter(partial_value, 'col', scatter_dimension=1, tiled=True)  75.3 us
    reduce_scatter x1, waiting for transfers between devices, previous_solution(): lax.psum_scatter(lax.dot_general(inverse_rows, prior_block, (((0,), (1,))...  68.1 us
    all_gather x1, blocking collectives, per_device(): lax.all_gather(solution_last.astype(jnp.bfloat16), 'col', axis=1, tiled=T...  24 us
    reduce_scatter x1, waiting for transfers between devices, per_device(): lax.psum_scatter(transposed_terms(inv_last, forward_last), 'row', scatter...  18.4 us
    unnamed x8, local copies, waits for them, and re-layouts  14.9 us
    all_gather x1, blocking collectives, per_device(): stacked = lax.all_gather(residue, 'row', axis=0, tiled=True)  13.3 us
    dot_general x1, matrix products, update_terms(): lax.dot_general(solution_half, factor, (((0,), (0,)), ((), ())), preferre...  11.2 us
  transfers between devices with their start and end apart: 4, of which 4 were waited for; matrix products, arithmetic and copies ran while one was open for 6% of the time, Pallas kernels for 0%

commit v1 on v0

v1 whole, which is shorter than its diff:
```python
import functools

import jax
import jax.numpy as jnp
from jax import lax
from jax.experimental import pallas as pl
from jax.experimental.pallas import tpu as pltpu
from jax.sharding import PartitionSpec as P

ROWS = 8
COLS = 16
RING = 4
ROUNDS = 31
SIDES = 512
SHARE = 512
BLOCK = 256
WIDE = 32
OWN = 64
LAG_ADD = 4
LAG_END = 8
SLOTS = LAG_END + 1
F32 = jnp.float32
BF16 = jnp.bfloat16


def remote(src, dst, send_sem, recv_sem, row, col):
    return pltpu.make_async_remote_copy(
        src_ref=src,
        dst_ref=dst,
        send_sem=send_sem,
        recv_sem=recv_sem,
        device_id=(row, col),
        device_id_type=pl.DeviceIdType.MESH,
    )


def each(start, stop, body):
    def step(index, carry):
        body(index)
        return carry

    lax.fori_loop(start, stop, step, 0)


def kernel(
    panel_hbm, known_hbm, rhs_hbm, inv_hbm, prev_hbm,
    upd_hbm, last_hbm, sol_prev_hbm,
    panel, known, rhs, inv, prev,
    acc, send_b, recv_b, part_c, send_e, recv_e, own_e, sol_out, sol_t,
    prod, half_out, half_up, half_dn, full_up_out, full_dn_out, full_up, full_dn,
    turn, upd, own_m, send_m, recv_m, prev_out,
    sem_panel, sem_known, sem_rhs, sem_inv, sem_prev, sem_out,
    swap_send, swap_recv, b_send, b_recv, c_send, c_recv, e_send, e_recv,
    pair_send, pair_recv, s_send, s_recv,
    half_send, half_recv, full_send, full_recv, m_send, m_recv, sem_upd,
):
    i = lax.axis_index("row")
    j = lax.axis_index("col")
    z = lax.div(i, 2)
    core = lax.rem(i, 2)
    mate = i + 1 - 2 * core
    z_up = lax.rem(z + 1, RING)
    z_dn = lax.rem(z + 3, RING)
    z_far = lax.rem(z + 2, RING)
    row_up = 2 * z_up + core
    row_dn = 2 * z_dn + core
    home = lax.rem(lax.div(j, 2), 2)

    def panel_load(k):
        return pltpu.make_async_copy(panel_hbm.at[k], panel.at[core, k], sem_panel.at[k])

    def known_load(h, k):
        cols = pl.ds(h * 256, 256)
        return pltpu.make_async_copy(
            known_hbm.at[k, :, cols], known.at[k, :, cols], sem_known.at[h, k]
        )

    def inv_load(b):
        cols = pl.ds(pl.multiple_of(b * SHARE, SHARE), SHARE)
        return pltpu.make_async_copy(inv_hbm.at[:, cols], inv.at[b], sem_inv.at[b])

    def prev_load(b):
        cols = pl.ds(pl.multiple_of(b * BLOCK, BLOCK), BLOCK)
        return pltpu.make_async_copy(prev_hbm.at[:, cols], prev.at[b], sem_prev.at[b])

    rhs_load = pltpu.make_async_copy(rhs_hbm, rhs, sem_rhs)

    @functools.partial(each, 0, ROUNDS)
    def _(k):
        panel_load(k).start()
        known_load(0, k).start()

    barrier = pltpu.get_barrier_semaphore()

    @functools.partial(each, 1, COLS)
    def _(d):
        pl.semaphore_signal(
            barrier, inc=1, device_id=(i, lax.rem(j + d, COLS)), device_id_type=pl.DeviceIdType.MESH
        )

    @functools.partial(each, 1, ROWS)
    def _(d):
        pl.semaphore_signal(
            barrier, inc=1, device_id=(lax.rem(i + d, ROWS), j), device_id_type=pl.DeviceIdType.MESH
        )

    @functools.partial(each, 0, ROUNDS)
    def _(k):
        known_load(1, k).start()

    rhs_load.start()
    blocks = 2 * z + 2

    @functools.partial(each, 0, blocks)
    def _(b):
        inv_load(b).start()

    @functools.partial(each, 0, j + 1)
    def _(b):
        prev_load(b).start()

    pl.semaphore_wait(barrier, COLS - 1 + ROWS - 1)

    def swap(k):
        return remote(
            panel.at[core, k], panel.at[core, k], swap_send.at[k], swap_recv.at[k], mate, j
        )

    def swap_in(k):
        other = 1 - core
        return remote(
            panel.at[other, k], panel.at[other, k], swap_send.at[k], swap_recv.at[k], mate, j
        )

    def b_copy(other):
        return remote(
            send_b.at[other], recv_b.at[j], b_send.at[other], b_recv.at[j], i, other
        )

    def b_in(other):
        return remote(
            send_b.at[other], recv_b.at[other], b_send.at[other], b_recv.at[other], i, other
        )

    for h in range(2):
        cols = pl.ds(h * 256, 256)

        def arrive(k):
            known_load(h, k).wait()
            if h == 0:
                panel_load(k).wait()
                swap(k).start()

        def product(k):
            return jnp.dot(panel[core, k], known[k, :, cols], preferred_element_type=F32)

        arrive(0)
        acc[...] = product(0)

        @functools.partial(each, 0, 10)
        def _(s):
            for u in range(3):
                arrive(3 * s + 1 + u)
            acc[...] += product(3 * s + 1) + product(3 * s + 2) + product(3 * s + 3)

        for g in range(2):
            flipped = acc[:, g * 128 : g * 128 + 128].T.astype(BF16)
            for u in range(4):
                send_b[8 * h + 4 * g + u] = flipped[u * WIDE : (u + 1) * WIDE]

        @functools.partial(each, 8 * h, 8 * h + 8)
        def _(other):
            @pl.when(other != j)
            def _():
                b_copy(other).start()

    rhs_load.wait()

    def subtract(d, total):
        other = lax.rem(j + d, COLS)
        b_in(other).wait_recv()
        return total - recv_b[other].astype(F32)

    residue = lax.fori_loop(1, COLS, subtract, rhs[...] - send_b[j].astype(F32))
    part_c[i] = residue.astype(BF16)

    def c_copy(other):
        return remote(part_c.at[i], part_c.at[i], c_send.at[other], c_recv.at[i], other, j)

    def c_in(other):
        return remote(part_c.at[other], part_c.at[other], c_send.at[other], c_recv.at[other], other, j)

    @functools.partial(each, 0, ROWS - 1 - i)
    def _(d):
        c_copy(ROWS - 1 - d).start()

    @functools.partial(each, 0, blocks)
    def _(b):
        inv_load(b).wait()

    def dot_t(left, right):
        return lax.dot_general(left, right, (((1,), (1,)), ((), ())), preferred_element_type=F32)

    def forward(d, total):
        other = i - d
        c_in(other).wait_recv()
        return total + dot_t(part_c[other], inv[other])

    forward_t = lax.fori_loop(1, i + 1, forward, dot_t(part_c[i], inv[i])).astype(BF16)

    def e_copy(chip):
        return remote(send_e.at[chip], recv_e.at[i], e_send.at[chip], e_recv.at[i], 2 * chip + home, j)

    def e_in(other):
        return remote(send_e.at[0], recv_e.at[other], e_send.at[0], e_recv.at[other], other, j)

    @functools.partial(each, 0, z + 1)
    def _(chip):
        left = jnp.dot(forward_t, inv[2 * chip], preferred_element_type=F32)
        right = jnp.dot(forward_t, inv[2 * chip + 1], preferred_element_type=F32)
        mine = jnp.logical_and(chip == z, core == home)

        @pl.when(mine)
        def _():
            own_e[:, :SHARE] = left
            own_e[:, SHARE:] = right

        @pl.when(jnp.logical_not(mine))
        def _():
            send_e[chip, :, :SHARE] = left.astype(BF16)
            send_e[chip, :, SHARE:] = right.astype(BF16)
            e_copy(chip).start()

    def pair_copy():
        return remote(
            sol_out.at[1 - core], sol_out.at[1 - core], pair_send, pair_recv, mate, j
        )

    def pair_in():
        return remote(sol_out.at[core], sol_out.at[core], pair_send, pair_recv, mate, j)

    out_last = pltpu.make_async_copy(sol_out.at[core], last_hbm, sem_out.at[0])

    def place(col):
        return lax.div(col, 4) * 2 + lax.rem(col, 2)

    def s_copy(other):
        spot = sol_t.at[place(j)]
        return remote(spot, spot, s_send.at[other], s_recv.at[place(j)], i, other)

    def s_in(slot):
        spot = sol_t.at[slot]
        return remote(spot, spot, s_send.at[0], s_recv.at[slot], i, lax.rem(j + 1, COLS))

    @pl.when(core == home)
    def _():
        own = own_e[...]

        def add_one(other, total):
            e_in(other).wait_recv()
            return total + recv_e[other].astype(F32)

        own = lax.fori_loop(2 * z, i, add_one, own)
        own = lax.fori_loop(i + 1, ROWS, add_one, own)
        sol_t[place(j)] = own.astype(BF16)

        @functools.partial(each, 1, COLS)
        def _(d):
            s_copy(lax.rem(j + d, COLS)).start()

        sol_out[0] = own[:, :SHARE]
        sol_out[1] = own[:, SHARE:]
        pair_copy().start()

    @pl.when(core != home)
    def _():
        pair_in().wait_recv()

    out_last.start()

    @functools.partial(each, 0, 8)
    def _(slot):
        @pl.when(jnp.logical_or(core != home, slot != place(j)))
        def _():
            s_in(slot).wait_recv()

    @functools.partial(each, 0, ROUNDS)
    def _(k):
        swap_in(k).wait_recv()

    def half_up_copy(t):
        return remote(
            half_out.at[t, 0:32], half_up.at[t], half_send.at[0, t], half_recv.at[0, t], row_up, j
        )

    def half_dn_copy(t):
        return remote(
            half_out.at[t, 32:64], half_dn.at[t], half_send.at[1, t], half_recv.at[1, t], row_dn, j
        )

    def full_up_copy(t):
        return remote(
            full_up_out.at[t], full_up.at[t], full_send.at[0, t], full_recv.at[0, t], row_up, j
        )

    def full_dn_copy(t):
        return remote(
            full_dn_out.at[t], full_dn.at[t], full_send.at[1, t], full_recv.at[1, t], row_dn, j
        )

    def upd_copy(t):
        k = lax.rem(t + ROUNDS - 1, ROUNDS)
        cols = pl.ds(pl.multiple_of(k * BLOCK, BLOCK), BLOCK)
        return pltpu.make_async_copy(upd.at[t], upd_hbm.at[:, cols], sem_upd.at[t])

    def rows_of(chip):
        return pl.ds(pl.multiple_of(chip * OWN, OWN), OWN)

    def first(t):
        k = lax.rem(t + ROUNDS - 1, ROUNDS)
        slot = lax.rem(t, SLOTS)
        left = sol_t[:, :, :SHARE].reshape(256, SHARE)
        right = sol_t[:, :, SHARE:].reshape(256, SHARE)
        prod[slot] = jnp.dot(left, panel[0, k], preferred_element_type=F32) + jnp.dot(
            right, panel[1, k], preferred_element_type=F32
        )
        half_out[t] = prod[slot, rows_of(z_far), :].astype(BF16)
        half_up_copy(t).start()
        half_dn_copy(t).start()

    def second(t):
        slot = lax.rem(t, SLOTS)
        half_up_copy(t).wait_recv()
        half_dn_copy(t).wait_recv()
        up = prod[slot, rows_of(z_up), :]
        full_up_out[t, 0:32] = (up[0:32] + half_up[t].astype(F32)).astype(BF16)
        full_up_out[t, 32:64] = up[32:64].astype(BF16)
        full_up_copy(t).start()
        dn = prod[slot, rows_of(z_dn), :]
        full_dn_out[t, 0:32] = dn[0:32].astype(BF16)
        full_dn_out[t, 32:64] = (dn[32:64] + half_dn[t].astype(F32)).astype(BF16)
        full_dn_copy(t).start()

    def third(t):
        k = lax.rem(t + ROUNDS - 1, ROUNDS)
        slot = lax.rem(t, SLOTS)
        block = known[k, :, pl.ds(pl.multiple_of(z * 128, 128), 128)]
        turn[...] = block.astype(F32).T
        full_up_copy(t).wait_recv()
        full_dn_copy(t).wait_recv()
        terms = prod[slot, rows_of(z), :] + full_up[t].astype(F32) + full_dn[t].astype(F32)
        upd[t] = turn[rows_of(core), :] - terms
        upd_copy(t).start()

    def step(t):
        @pl.when(t < ROUNDS)
        def _():
            first(t)

        @pl.when(jnp.logical_and(t >= LAG_ADD, t < ROUNDS + LAG_ADD))
        def _():
            second(t - LAG_ADD)

        @pl.when(t >= LAG_END)
        def _():
            third(t - LAG_END)

    each(0, LAG_END + 1, step)

    def m_copy(other):
        return remote(send_m.at[other], recv_m.at[j], m_send.at[other], m_recv.at[j], i, other)

    def m_in(other):
        return remote(send_m.at[other], recv_m.at[other], m_send.at[other], m_recv.at[other], i, other)

    @functools.partial(each, 0, j + 1)
    def _(b):
        prev_load(b).wait()

    prior = upd[0].astype(BF16)
    own_m[...] = jnp.dot(prior, prev[j], preferred_element_type=F32)

    @functools.partial(each, 0, j)
    def _(b):
        send_m[b] = jnp.dot(prior, prev[b], preferred_element_type=F32).astype(BF16)
        m_copy(b).start()

    each(LAG_END + 1, ROUNDS + LAG_END, step)

    def add_m(other, total):
        m_in(other).wait_recv()
        return total + recv_m[other].astype(F32)

    prev_out[...] = lax.fori_loop(j + 1, COLS, add_m, own_m[...])
    out_prev = pltpu.make_async_copy(prev_out, sol_prev_hbm, sem_out.at[1])
    out_prev.start()

    @functools.partial(each, 0, COLS)
    def _(other):
        @pl.when(other != j)
        def _():
            b_copy(other).wait_send()

            @pl.when(core == home)
            def _():
                s_copy(other).wait_send()

    @functools.partial(each, 0, ROWS - 1 - i)
    def _(d):
        c_copy(ROWS - 1 - d).wait_send()

    @functools.partial(each, 0, z + 1)
    def _(chip):
        @pl.when(jnp.logical_not(jnp.logical_and(chip == z, core == home)))
        def _():
            e_copy(chip).wait_send()

    @pl.when(core == home)
    def _():
        pair_copy().wait_send()

    @functools.partial(each, 0, j)
    def _(b):
        m_copy(b).wait_send()

    @functools.partial(each, 0, ROUNDS)
    def _(t):
        swap(t).wait_send()
        half_up_copy(t).wait_send()
        half_dn_copy(t).wait_send()
        full_up_copy(t).wait_send()
        full_dn_copy(t).wait_send()
        upd_copy(t).wait()

    out_last.wait()
    out_prev.wait()


def scratch():
    dma = pltpu.SemaphoreType.DMA
    return [
        pltpu.VMEM((2, ROUNDS, SHARE, BLOCK), BF16),
        pltpu.VMEM((ROUNDS, BLOCK, SIDES), BF16),
        pltpu.VMEM((WIDE, SHARE), F32),
        pltpu.VMEM((ROWS, SHARE, SHARE), BF16),
        pltpu.VMEM((COLS, BLOCK, BLOCK), BF16),
        pltpu.VMEM((SHARE, 256), F32),
        pltpu.VMEM((COLS, WIDE, SHARE), BF16),
        pltpu.VMEM((COLS, WIDE, SHARE), BF16),
        pltpu.VMEM((ROWS, WIDE, SHARE), BF16),
        pltpu.VMEM((RING, WIDE, 2 * SHARE), BF16),
        pltpu.VMEM((ROWS, WIDE, 2 * SHARE), BF16),
        pltpu.VMEM((WIDE, 2 * SHARE), F32),
        pltpu.VMEM((2, WIDE, SHARE), F32),
        pltpu.VMEM((8, WIDE, 2 * SHARE), BF16),
        pltpu.VMEM((SLOTS, 256, BLOCK), F32),
        pltpu.VMEM((ROUNDS, OWN, BLOCK), BF16),
        pltpu.VMEM((ROUNDS, OWN // 2, BLOCK), BF16),
        pltpu.VMEM((ROUNDS, OWN // 2, BLOCK), BF16),
        pltpu.VMEM((ROUNDS, OWN, BLOCK), BF16),
        pltpu.VMEM((ROUNDS, OWN, BLOCK), BF16),
        pltpu.VMEM((ROUNDS, OWN, BLOCK), BF16),
        pltpu.VMEM((ROUNDS, OWN, BLOCK), BF16),
        pltpu.VMEM((128, BLOCK), F32),
        pltpu.VMEM((ROUNDS, OWN, BLOCK), F32),
        pltpu.VMEM((OWN, BLOCK), F32),
        pltpu.VMEM((COLS, OWN, BLOCK), BF16),
        pltpu.VMEM((COLS, OWN, BLOCK), BF16),
        pltpu.VMEM((OWN, BLOCK), F32),
        dma((ROUNDS,)),
        dma((2, ROUNDS)),
        dma(()),
        dma((ROWS,)),
        dma((COLS,)),
        dma((2,)),
        dma((ROUNDS,)),
        dma((ROUNDS,)),
        dma((COLS,)),
        dma((COLS,)),
        dma((ROWS,)),
        dma((ROWS,)),
        dma((RING,)),
        dma((ROWS,)),
        dma(()),
        dma(()),
        dma((COLS,)),
        dma((8,)),
        dma((2, ROUNDS)),
        dma((2, ROUNDS)),
        dma((2, ROUNDS)),
        dma((2, ROUNDS)),
        dma((COLS,)),
        dma((COLS,)),
        dma((ROUNDS,)),
    ]


def per_device(factor_panel, solved_prev, rhs_last, inv_last, inv_prev):
    panel = factor_panel.transpose(1, 2, 0, 3).reshape(ROUNDS, SHARE, BLOCK)
    known = solved_prev.reshape(ROUNDS, BLOCK, SIDES)
    anywhere = pl.BlockSpec(memory_space=pl.ANY)
    updated, last_t, prev_t = pl.pallas_call(
        kernel,
        out_shape=[
            jax.ShapeDtypeStruct((OWN, ROUNDS * BLOCK), F32),
            jax.ShapeDtypeStruct((WIDE, SHARE), F32),
            jax.ShapeDtypeStruct((OWN, BLOCK), F32),
        ],
        in_specs=[anywhere] * 5,
        out_specs=[anywhere] * 3,
        scratch_shapes=scratch(),
        compiler_params=pltpu.CompilerParams(
            collective_id=0, has_side_effects=True, vmem_limit_bytes=60 * 1024 * 1024
        ),
        cost_estimate=pl.CostEstimate(
            flops=9 * 10**9, bytes_accessed=21 * 10**6, transcendentals=0
        ),
    )(panel, known, rhs_last.T, inv_last, inv_prev.reshape(BLOCK, COLS * BLOCK))
    return updated.reshape(OWN, ROUNDS, 1, BLOCK), last_t.T, prev_t.T


def solution(mesh):
    in_specs = (
        P("row", None, "col", None),
        P(None, "col", None, None),
        P("row", "col"),
        P("row", None),
        P(None, "col", None, None),
    )
    out_specs = (P("row", None, "col", None), P("row", "col"), P("col", "row"))
    return jax.shard_map(
        per_device, mesh=mesh, in_specs=in_specs, out_specs=out_specs, check_vma=False
    )
```

time: 351 us -> 94.3 us (0.27)
  waiting for transfers between devices: 243 us -> 0 us
  Pallas kernels: 0 us -> 85.8 us
  blocking collectives: 37.3 us -> 0 us
  matrix products: 30.2 us -> 0 us
  local copies, waits for them, and re-layouts: 22.6 us -> 6.42 us
  between operations: 13.8 us -> 0.65 us
    reduce_scatter x4 -> x0, waiting for transfers between devices: 243 us -> none  [the longest x1 80.7 us: per_device(): lax.psum_scatter(update_terms(solution_half, factor), 'row', scatter_dime...]
    pallas_call x0 -> x1, Pallas kernels: none -> 85.8 us  [per_device(): pl.pallas_call(kernel, out_shape=[jax.ShapeDtypeStruct((OWN, ROUNDS * BLO...]
    all_gather x2 -> x0, blocking collectives: 37.3 us -> none  [the longest x1 24 us: per_device(): lax.all_gather(solution_last.astype(jnp.bfloat16), 'col', axis=1, tiled=T...]
    dot_general x4 -> x0, matrix products: 30.2 us -> none  [the longest x1 11.2 us: update_terms(): lax.dot_general(solution_half, factor, (((0,), (0,)), ((), ())), preferre...]
    unnamed x8 -> x4, local copies, waits for them, and re-layouts: 14.9 us -> 2.11 us
  transfers between devices with their start and end apart: 4 -> 0, of which waited for: 4 -> 0; matrix products, arithmetic and copies ran while one was open for 6% -> 0% of each run, Pallas kernels for 0% -> 0%
where the time goes in v1:
time: 94.3 us; the launch traced here: 92.8 us
  Pallas kernels  85.8 us (91%)
  local copies, waits for them, and re-layouts  6.42 us (7%)
    pallas_call x1, Pallas kernels, per_device(): pl.pallas_call(kernel, out_shape=[jax.ShapeDtypeStruct((OWN, ROUNDS * BLO...  85.8 us
    reshape x1, local copies, waits for them, and re-layouts, per_device(): return (updated.reshape(OWN, ROUNDS, 1, BLOCK), last_t.T, prev_t.T)  4.31 us
    unnamed x4, local copies, waits for them, and re-layouts  2.11 us

profile of v1, /device:TPU:0, one launch (start us, length us, event | category | flops | bytes accessed | tf_op | source)
XLA Modules:
  0.0 92.8 jit_solution(1846808997314846595)
XLA Ops:
  0.6 85.8 %shard_map.76 = (f32[64,7936]{1,0:T(8,128)}, f32[32,512]{1,0:T(8,128)}, f32[64,256]{1,0:T(8,128)}) custom-call(bf16[31,512,256]{2,1,0:T(8,128)(2,1)} %bitcast.12, bf16[31,256,512]{2,1,0:T(8,128)(2,1)} %bitcast.13, f32[32,512]{1,0:T(8,128)} %bitcast.15, bf16[512,4096]{1,0:T(8,128)(2,1)} %inv_hbm.1, bf16[256,4096]{1,0:T(8,128)(2,1)} %bitcast.14), custom_call_target="tpu_custom_call" | custom-call | flops 8999999488 | bytes 21000000 | tf_op jit(solution)/shard_map/pallas_call | solution.py:502
  86.4 0.0 copy-start
  86.4 4.3 %reshape.22 = f32[64,31,1,256]{3,2,1,0:T(1,128)} reshape(f32[64,7936]{1,0:T(8,128)} %get-tuple-element.6) | data formatting | bytes 4063232 | tf_op jit(solution)/shard_map/reshape | solution.py:519
  90.7 1.5 %copy.14 = f32[512,32]{0,1:T(8,128)} copy(f32[512,32]{0,1:T(8,128)} %bitcast.11) | data formatting | bytes 131072
  92.2 0.0 copy-done
  92.2 0.6 copy.15
Async XLA Ops:
  86.4 5.8 %copy-start = (f32[64,256]{1,0:T(8,128)S(1)}, f32[64,256]{1,0:T(8,128)}, u32[]{:S(2)}) copy-start(f32[64,256]{1,0:T(8,128)} %get-tuple-element.8) | copy-start | bytes 196612

commit v2 on v1

v2 whole, which is shorter than its diff:
```python
import functools

import jax
import jax.numpy as jnp
from jax import lax
from jax.experimental import pallas as pl
from jax.experimental.pallas import tpu as pltpu
from jax.sharding import PartitionSpec as P

ROWS = 8
COLS = 16
RING = 4
ROUNDS = 31
SIDES = 512
SHARE = 512
BLOCK = 256
WIDE = 32
OWN = 64
GROUP = 6
STEPS = 2 * ROUNDS
AHEAD = 12
LAG_ADD = 6
LAG_END = 12
SLOTS = LAG_END + 2
PIECES = 4
GROUPS = 5
F32 = jnp.float32
BF16 = jnp.bfloat16


def remote(src, dst, send_sem, recv_sem, row, col):
    return pltpu.make_async_remote_copy(
        src_ref=src,
        dst_ref=dst,
        send_sem=send_sem,
        recv_sem=recv_sem,
        device_id=(row, col),
        device_id_type=pl.DeviceIdType.MESH,
    )


def each(start, stop, body):
    def step(index, carry):
        body(index)
        return carry

    lax.fori_loop(start, stop, step, 0)


def kernel(
    panel_hbm, known_hbm, rhs_hbm, inv_hbm, prev_hbm,
    upd_hbm, last_hbm, sol_prev_hbm,
    panel, known, rhs, inv, prev,
    acc, send_b, recv_b, part_c, send_e, recv_e, own_e, sol_out, sol_t,
    prod, half_out, half_in, full_out, full_in,
    turn, begin, upd, prior, own_m, send_m, recv_m, prev_out,
    sem_panel, sem_known, sem_rhs, sem_inv, sem_prev, sem_out,
    swap_send, swap_recv, b_send, b_recv, c_send, c_recv, e_send, e_recv,
    pair_send, pair_recv, s_send, s_recv,
    half_send, half_recv, full_send, full_recv, m_send, m_recv, sem_upd,
):
    i = lax.axis_index("row")
    j = lax.axis_index("col")
    z = lax.div(i, 2)
    core = lax.rem(i, 2)
    mate = i + 1 - 2 * core
    z_up = lax.rem(z + 1, RING)
    z_dn = lax.rem(z + 3, RING)
    z_far = lax.rem(z + 2, RING)
    row_up = 2 * z_up + core
    row_dn = 2 * z_dn + core
    home = lax.rem(lax.div(j, 2), 2)

    def span(g):
        return pl.ds((ROUNDS - 1) if isinstance(g, str) else g * GROUP, 1 if isinstance(g, str) else GROUP)

    def sem_of(g):
        return GROUPS if isinstance(g, str) else g

    def panel_load(h, g):
        rows = pl.ds(h * 256, 256)
        return pltpu.make_async_copy(
            panel_hbm.at[span(g), rows],
            panel.at[core, span(g), rows],
            sem_panel.at[h, sem_of(g)],
        )

    def known_load(g):
        return pltpu.make_async_copy(
            known_hbm.at[span(g)], known.at[span(g)], sem_known.at[sem_of(g)]
        )

    inv_load = pltpu.make_async_copy(inv_hbm, inv, sem_inv)
    prev_load = pltpu.make_async_copy(prev_hbm, prev, sem_prev)
    rhs_load = pltpu.make_async_copy(rhs_hbm, rhs, sem_rhs)

    panel_load(0, "last").start()
    known_load("last").start()

    @functools.partial(each, 0, GROUPS)
    def _(g):
        panel_load(0, g).start()
        known_load(g).start()

    barrier = pltpu.get_barrier_semaphore()

    @functools.partial(each, 1, COLS)
    def _(d):
        pl.semaphore_signal(
            barrier, inc=1, device_id=(i, lax.rem(j + d, COLS)), device_id_type=pl.DeviceIdType.MESH
        )

    @functools.partial(each, 1, ROWS)
    def _(d):
        pl.semaphore_signal(
            barrier, inc=1, device_id=(lax.rem(i + d, ROWS), j), device_id_type=pl.DeviceIdType.MESH
        )

    panel_load(1, "last").start()

    @functools.partial(each, 0, GROUPS)
    def _(g):
        panel_load(1, g).start()

    rhs_load.start()

    def swap(h, g):
        spot = panel.at[core, span(g), pl.ds(h * 256, 256)]
        return remote(spot, spot, swap_send, swap_recv.at[sem_of(g)], mate, j)

    def swap_in(g):
        spot = panel.at[1 - core, span(g)]
        return remote(spot, spot, swap_send, swap_recv.at[sem_of(g)], mate, j)

    def swap_all():
        return remote(panel.at[core], panel.at[core], swap_send, swap_recv.at[0], mate, j)

    def b_copy(h, other):
        return remote(
            send_b.at[h, other], recv_b.at[h, j], b_send, b_recv.at[h], i, other
        )

    def b_all(h):
        rest = pl.ds(0, COLS - 1)
        return remote(
            send_b.at[h, rest], recv_b.at[h, rest], b_send, b_recv.at[h], i, lax.rem(j + 1, COLS)
        )

    for h in range(2):
        rows = pl.ds(h * 256, 256)

        def arrive(g):
            panel_load(h, g).wait()
            if h == 0:
                known_load(g).wait()
            else:
                swap(1, g).start()

        def product(k):
            return jnp.dot(panel[core, k, rows], known[k], preferred_element_type=F32)

        arrive("last")
        acc[...] = product(ROUNDS - 1)

        @functools.partial(each, 0, GROUPS)
        def _(g):
            arrive(g)
            total = product(GROUP * g)
            for u in range(1, GROUP):
                total = total + product(GROUP * g + u)
            acc[...] += total

        for g in range(4):
            flipped = acc[:, g * 128 : g * 128 + 128].T.astype(BF16)
            for u in range(4):
                send_b[h, 4 * g + u] = flipped[u * WIDE : (u + 1) * WIDE]

        if h == 0:
            pl.semaphore_wait(barrier, COLS - 1 + ROWS - 1)

        for odd in range(2):

            @functools.partial(each, 0, COLS // 2)
            def _(half):
                other = 2 * half + odd

                @pl.when(other != j)
                def _():
                    b_copy(h, other).start()

        if h == 0:
            swap(0, "last").start()

            @functools.partial(each, 0, GROUPS)
            def _(g):
                swap(0, g).start()

            inv_load.start()
            prev_load.start()

    rhs_load.wait()

    for h in range(2):
        rows = pl.ds(h * 256, 256)

        def subtract(d, total):
            other = lax.rem(j + d, COLS)
            return total - recv_b[h, other].astype(F32)

        b_all(h).wait_recv()
        residue = lax.fori_loop(1, COLS, subtract, rhs[:, rows] - send_b[h, j].astype(F32))
        part_c[i, :, rows] = residue.astype(BF16)

    def c_copy(other):
        return remote(part_c.at[i], part_c.at[i], c_send.at[other], c_recv.at[i], other, j)

    def c_in(other):
        return remote(part_c.at[other], part_c.at[other], c_send.at[other], c_recv.at[other], other, j)

    @functools.partial(each, 0, ROWS - 1 - i)
    def _(d):
        c_copy(ROWS - 1 - d).start()

    inv_load.wait()

    def inv_block(b):
        return inv[:, pl.ds(pl.multiple_of(b * SHARE, SHARE), SHARE)]

    def dot_t(left, right):
        return lax.dot_general(left, right, (((1,), (1,)), ((), ())), preferred_element_type=F32)

    def forward(d, total):
        other = i - d
        c_in(other).wait_recv()
        return total + dot_t(part_c[other], inv_block(other))

    forward_t = lax.fori_loop(1, i + 1, forward, dot_t(part_c[i], inv_block(i))).astype(BF16)

    def e_copy(chip):
        return remote(send_e.at[chip], recv_e.at[i], e_send.at[chip], e_recv.at[i], 2 * chip + home, j)

    def e_in(other):
        return remote(send_e.at[0], recv_e.at[other], e_send.at[0], e_recv.at[other], other, j)

    @functools.partial(each, 0, z + 1)
    def _(chip):
        left = jnp.dot(forward_t, inv_block(2 * chip), preferred_element_type=F32)
        right = jnp.dot(forward_t, inv_block(2 * chip + 1), preferred_element_type=F32)
        mine = jnp.logical_and(chip == z, core == home)

        @pl.when(mine)
        def _():
            own_e[:, :SHARE] = left
            own_e[:, SHARE:] = right

        @pl.when(jnp.logical_not(mine))
        def _():
            send_e[chip, :, :SHARE] = left.astype(BF16)
            send_e[chip, :, SHARE:] = right.astype(BF16)
            e_copy(chip).start()

    def pair_copy():
        return remote(
            sol_out.at[1 - core], sol_out.at[1 - core], pair_send, pair_recv, mate, j
        )

    def pair_in():
        return remote(sol_out.at[core], sol_out.at[core], pair_send, pair_recv, mate, j)

    out_last = pltpu.make_async_copy(sol_out.at[core], last_hbm, sem_out.at[0])

    my_set = lax.rem(j, 2)
    my_chip = lax.div(j, 4)

    def s_copy(other):
        spot = sol_t.at[my_set, my_chip]
        return remote(spot, spot, s_send, s_recv.at[my_set, my_chip], i, other)

    def s_in(side, chip):
        spot = sol_t.at[side, chip]
        return remote(
            spot, spot, s_send, s_recv.at[side, chip], i, lax.rem(j + 1, COLS)
        )

    @pl.when(core == home)
    def _():
        own = own_e[...]

        def add_one(other, total):
            e_in(other).wait_recv()
            return total + recv_e[other].astype(F32)

        own = lax.fori_loop(2 * z, i, add_one, own)
        own = lax.fori_loop(i + 1, ROWS, add_one, own)
        sol_t[my_set, my_chip] = own.astype(BF16)

        @functools.partial(each, 1, COLS)
        def _(d):
            s_copy(lax.rem(j + d, COLS)).start()

        sol_out[0] = own[:, :SHARE]
        sol_out[1] = own[:, SHARE:]
        pair_copy().start()

    @pl.when(core != home)
    def _():
        pair_in().wait_recv()

    out_last.start()

    def solved(side):
        @functools.partial(each, 0, RING)
        def _(chip):
            @pl.when((core != home) | (my_set != side) | (my_chip != chip))
            def _():
                s_in(side, chip).wait_recv()

    def half_copy(t, up):
        n = lax.rem(t, SLOTS)
        return remote(
            half_out.at[n, up], half_in.at[n, up], half_send.at[n], half_recv.at[n],
            row_up if up else row_dn, j,
        )

    def half_both(t):
        n = lax.rem(t, SLOTS)
        return remote(half_out.at[n], half_in.at[n], half_send.at[n], half_recv.at[n], row_up, j)

    def full_copy(t, up):
        n = lax.rem(t, SLOTS)
        return remote(
            full_out.at[n, up], full_in.at[n, up], full_send.at[n], full_recv.at[n],
            row_up if up else row_dn, j,
        )

    def full_both(t):
        n = lax.rem(t, SLOTS)
        return remote(full_out.at[n], full_in.at[n], full_send.at[n], full_recv.at[n], row_up, j)

    def side_of(t):
        late = lax.rem(lax.max(t - 2 * AHEAD, 0), 2)
        return jnp.where(t < 2 * AHEAD, lax.div(t, AHEAD), late)

    def spot_of(t):
        late = AHEAD + lax.div(lax.max(t - 2 * AHEAD, 0), 2)
        return jnp.where(t < 2 * AHEAD, lax.rem(t, AHEAD), late)

    def round_of(spot):
        return lax.rem(spot + ROUNDS - 1, ROUNDS)

    def sides_of(side):
        return pl.ds(pl.multiple_of(side * WIDE, WIDE), WIDE)

    def rows_of(chip):
        return pl.ds(pl.multiple_of(chip * WIDE, WIDE), WIDE)

    def swapped(t):
        spot = spot_of(t)

        @pl.when(spot == 0)
        def _():
            swap_in("last").wait_recv()

        @pl.when((spot > 0) & (lax.rem(spot + GROUP - 1, GROUP) == 0))
        def _():
            swap_in(lax.div(spot - 1, GROUP)).wait_recv()

    def multiply(t, side):
        k = round_of(spot_of(t))
        left = sol_t[side, :, :, :SHARE].reshape(RING * WIDE, SHARE)
        right = sol_t[side, :, :, SHARE:].reshape(RING * WIDE, SHARE)
        return jnp.dot(left, panel[0, k], preferred_element_type=F32) + jnp.dot(
            right, panel[1, k], preferred_element_type=F32
        )

    def multiply_both(t):
        k = round_of(spot_of(t))
        left = sol_t[:, :, :, :SHARE].reshape(2 * RING * WIDE, SHARE)
        right = sol_t[:, :, :, SHARE:].reshape(2 * RING * WIDE, SHARE)
        return jnp.dot(left, panel[0, k], preferred_element_type=F32) + jnp.dot(
            right, panel[1, k], preferred_element_type=F32
        )

    def first(t):
        n = lax.rem(t, SLOTS)

        @pl.when(side_of(t) == 0)
        def _():
            swapped(t)

        @pl.when(t < 2 * AHEAD)
        def _():
            prod[n] = multiply(t, side_of(t))

        @pl.when((t >= 2 * AHEAD) & (side_of(t) == 0))
        def _():
            both = multiply_both(t)
            prod[n] = both[: RING * WIDE]
            prod[lax.rem(t + 1, SLOTS)] = both[RING * WIDE :]

        @pl.when(t >= SLOTS)
        def _():
            half_both(t).wait_send()

        far = prod[n, rows_of(z_far), :].astype(BF16)
        half_out[n, 1] = far[:16]
        half_out[n, 0] = far[16:]
        half_copy(t, 1).start()
        half_copy(t, 0).start()

    def second(t):
        n = lax.rem(t, SLOTS)
        half_both(t).wait_recv()

        @pl.when(t >= SLOTS)
        def _():
            full_both(t).wait_send()

        up = prod[n, rows_of(z_up), :]
        full_out[n, 1, 0:16] = (up[0:16] + half_in[n, 1].astype(F32)).astype(BF16)
        full_out[n, 1, 16:32] = up[16:32].astype(BF16)
        full_copy(t, 1).start()
        dn = prod[n, rows_of(z_dn), :]
        full_out[n, 0, 0:16] = dn[0:16].astype(BF16)
        full_out[n, 0, 16:32] = (dn[16:32] + half_in[n, 0].astype(F32)).astype(BF16)
        full_copy(t, 0).start()

    def third(t):
        side, spot = side_of(t), spot_of(t)
        k = round_of(spot)
        n = lax.rem(t, SLOTS)

        @pl.when(side == 0)
        def _():
            block = known[k, :, pl.ds(pl.multiple_of(z * 128, 128), 128)]
            turn[...] = block.astype(F32).T
            begin[spot] = turn[pl.ds(pl.multiple_of(core * OWN, OWN), OWN), :]

        full_both(t).wait_recv()
        sides = sides_of(side)
        terms = prod[n, rows_of(z), :] + full_in[n, 1].astype(F32) + full_in[n, 0].astype(F32)
        done = begin[spot, sides, :] - terms
        for part in range(2):
            where = side * (WIDE * 2 * ROUNDS) + 2 * k + part
            upd[pl.ds(where, WIDE, stride=2 * ROUNDS), :] = done[:, part * 128 : part * 128 + 128]

        @pl.when(spot == 0)
        def _():
            prior[sides, :] = done.astype(BF16)

    def step(t):
        @pl.when(t < STEPS)
        def _():
            first(t)

        @pl.when(jnp.logical_and(t >= LAG_ADD, t < STEPS + LAG_ADD))
        def _():
            second(t - LAG_ADD)

        @pl.when(t >= LAG_END)
        def _():
            third(t - LAG_END)

    solved(0)
    each(0, AHEAD, step)
    solved(1)
    each(AHEAD, AHEAD + LAG_END + 1, step)

    def m_copy(other):
        return remote(send_m.at[other], recv_m.at[j], m_send.at[other], m_recv.at[j], i, other)

    def m_in(other):
        return remote(send_m.at[other], recv_m.at[other], m_send.at[other], m_recv.at[other], i, other)

    prev_load.wait()

    def prev_block(b):
        return prev[:, pl.ds(pl.multiple_of(b * BLOCK, BLOCK), BLOCK)]

    own_m[...] = jnp.dot(prior[...], prev_block(j), preferred_element_type=F32)

    @functools.partial(each, 0, j)
    def _(b):
        send_m[b] = jnp.dot(prior[...], prev_block(b), preferred_element_type=F32).astype(BF16)
        m_copy(b).start()

    each(AHEAD + LAG_END + 1, STEPS + LAG_END, step)

    out_upd = pltpu.make_async_copy(upd, upd_hbm, sem_upd)
    out_upd.start()

    def add_m(other, total):
        m_in(other).wait_recv()
        return total + recv_m[other].astype(F32)

    prev_out[...] = lax.fori_loop(j + 1, COLS, add_m, own_m[...])
    out_prev = pltpu.make_async_copy(prev_out, sol_prev_hbm, sem_out.at[1])
    out_prev.start()

    b_all(0).wait_send()
    b_all(1).wait_send()
    swap_all().wait_send()

    @functools.partial(each, 0, ROWS - 1 - i)
    def _(d):
        c_copy(ROWS - 1 - d).wait_send()

    @functools.partial(each, 0, z + 1)
    def _(chip):
        @pl.when(jnp.logical_not(jnp.logical_and(chip == z, core == home)))
        def _():
            e_copy(chip).wait_send()

    @pl.when(core == home)
    def _():
        pair_copy().wait_send()

        @functools.partial(each, 1, COLS)
        def _(d):
            s_copy(lax.rem(j + d, COLS)).wait_send()

    @functools.partial(each, 0, j)
    def _(b):
        m_copy(b).wait_send()

    @functools.partial(each, STEPS - SLOTS, STEPS)
    def _(t):
        half_both(t).wait_send()
        full_both(t).wait_send()

    out_upd.wait()
    out_last.wait()
    out_prev.wait()


def hand_over(upd_in, last_in, prev_in, upd_out, last_out, prev_out, upd, last, prev, sems):
    def piece(ref, n):
        rows = ref.shape[0] // PIECES
        return ref.at[pl.ds(n * rows, rows)]

    moves = [(last_in, last, last_out), (prev_in, prev, prev_out)]
    moves += [(piece(upd_in, n), piece(upd, n), piece(upd_out, n)) for n in range(PIECES)]
    loads = [pltpu.make_async_copy(a, b, sems.at[0, n]) for n, (a, b, _) in enumerate(moves)]
    stores = [pltpu.make_async_copy(b, c, sems.at[1, n]) for n, (_, b, c) in enumerate(moves)]
    for load in loads:
        load.start()
    for load, store in zip(loads, stores):
        load.wait()
        store.start()
    for store in stores:
        store.wait()


def scratch():
    dma = pltpu.SemaphoreType.DMA
    return [
        pltpu.VMEM((2, ROUNDS, SHARE, BLOCK), BF16),
        pltpu.VMEM((ROUNDS, BLOCK, SIDES), BF16),
        pltpu.VMEM((WIDE, SHARE), F32),
        pltpu.VMEM((SHARE, ROWS * SHARE), BF16),
        pltpu.VMEM((BLOCK, COLS * BLOCK), BF16),
        pltpu.VMEM((256, SIDES), F32),
        pltpu.VMEM((2, COLS, WIDE, 256), BF16),
        pltpu.VMEM((2, COLS, WIDE, 256), BF16),
        pltpu.VMEM((ROWS, WIDE, SHARE), BF16),
        pltpu.VMEM((RING, WIDE, 2 * SHARE), BF16),
        pltpu.VMEM((ROWS, WIDE, 2 * SHARE), BF16),
        pltpu.VMEM((WIDE, 2 * SHARE), F32),
        pltpu.VMEM((2, WIDE, SHARE), F32),
        pltpu.VMEM((2, RING, WIDE, 2 * SHARE), BF16),
        pltpu.VMEM((SLOTS, RING * WIDE, BLOCK), F32),
        pltpu.VMEM((SLOTS, 2, WIDE // 2, BLOCK), BF16),
        pltpu.VMEM((SLOTS, 2, WIDE // 2, BLOCK), BF16),
        pltpu.VMEM((SLOTS, 2, WIDE, BLOCK), BF16),
        pltpu.VMEM((SLOTS, 2, WIDE, BLOCK), BF16),
        pltpu.VMEM((128, BLOCK), F32),
        pltpu.VMEM((ROUNDS, OWN, BLOCK), F32),
        pltpu.VMEM((OWN * ROUNDS * 2, 128), F32),
        pltpu.VMEM((OWN, BLOCK), BF16),
        pltpu.VMEM((OWN, BLOCK), F32),
        pltpu.VMEM((COLS, OWN, BLOCK), BF16),
        pltpu.VMEM((COLS, OWN, BLOCK), BF16),
        pltpu.VMEM((OWN, BLOCK), F32),
        dma((2, GROUPS + 1)),
        dma((GROUPS + 1,)),
        dma(()),
        dma(()),
        dma(()),
        dma((2,)),
        dma(()),
        dma((GROUPS + 1,)),
        dma(()),
        dma((2,)),
        dma((ROWS,)),
        dma((ROWS,)),
        dma((RING,)),
        dma((ROWS,)),
        dma(()),
        dma(()),
        dma(()),
        dma((2, RING)),
        dma((SLOTS,)),
        dma((SLOTS,)),
        dma((SLOTS,)),
        dma((SLOTS,)),
        dma((COLS,)),
        dma((COLS,)),
        dma(()),
    ]


def per_device(factor_panel, solved_prev, rhs_last, inv_last, inv_prev):
    panel = factor_panel.transpose(1, 2, 0, 3).reshape(ROUNDS, SHARE, BLOCK)
    known = solved_prev.reshape(ROUNDS, BLOCK, SIDES)
    anywhere = pl.BlockSpec(memory_space=pl.ANY)
    out_shape = [
        jax.ShapeDtypeStruct((OWN * ROUNDS * 2, 128), F32),
        jax.ShapeDtypeStruct((WIDE, SHARE), F32),
        jax.ShapeDtypeStruct((OWN, BLOCK), F32),
    ]
    results = pl.pallas_call(
        kernel,
        out_shape=out_shape,
        in_specs=[anywhere] * 5,
        out_specs=[anywhere] * 3,
        scratch_shapes=scratch(),
        compiler_params=pltpu.CompilerParams(
            collective_id=0, has_side_effects=True, vmem_limit_bytes=60 * 1024 * 1024
        ),
        cost_estimate=pl.CostEstimate(
            flops=9 * 10**9, bytes_accessed=21 * 10**6, transcendentals=0
        ),
    )(panel, known, rhs_last.T, inv_last, inv_prev.reshape(BLOCK, COLS * BLOCK))
    updated, last_t, prev_t = pl.pallas_call(
        hand_over,
        out_shape=out_shape,
        in_specs=[anywhere] * 3,
        out_specs=[anywhere] * 3,
        scratch_shapes=[pltpu.VMEM(shape.shape, shape.dtype) for shape in out_shape]
        + [pltpu.SemaphoreType.DMA((2, PIECES + 2))],
        compiler_params=pltpu.CompilerParams(vmem_limit_bytes=60 * 1024 * 1024),
    )(*results)
    return updated.reshape(OWN, ROUNDS, 1, BLOCK), last_t.T, prev_t.T


def solution(mesh):
    in_specs = (
        P("row", None, "col", None),
        P(None, "col", None, None),
        P("row", "col"),
        P("row", None),
        P(None, "col", None, None),
    )
    out_specs = (P("row", None, "col", None), P("row", "col"), P("col", "row"))
    return jax.shard_map(
        per_device, mesh=mesh, in_specs=in_specs, out_specs=out_specs, check_vma=False
    )
```

time: 94.3 us -> 84.6 us (0.90)
  the two profiles are of different devices: /device:TPU:0 before, /device:TPU:28 now
where the time goes in v2:
time: 84.6 us; the launch traced here: 84.5 us
  Pallas kernels  83.8 us (99%)
    pallas_call x1, Pallas kernels, per_device(): pl.pallas_call(kernel, out_shape=out_shape, in_specs=[anywhere] * 5, out_...  81.3 us
    pallas_call x1, Pallas kernels, per_device(): pl.pallas_call(hand_over, out_shape=out_shape, in_specs=[anywhere] * 3, o...  2.5 us

profile of v2, /device:TPU:28, one launch (start us, length us, event | category | flops | bytes accessed | tf_op | source)
XLA Modules:
  0.0 84.5 jit_solution(14918864682194486083)
XLA Ops:
  0.6 81.3 %shard_map.76 = (f32[3968,128]{1,0:T(8,128)}, f32[32,512]{1,0:T(8,128)}, f32[64,256]{1,0:T(8,128)}) custom-call(bf16[31,512,256]{2,1,0:T(8,128)(2,1)} %bitcast.11, bf16[31,256,512]{2,1,0:T(8,128)(2,1)} %bitcast.12, f32[32,512]{1,0:T(8,128)} %bitcast.15, bf16[512,4096]{1,0:T(8,128)(2,1)} %inv_hbm.1, bf16[256,4096]{1,0:T(8,128)(2,1)} %bitcast.13), custom_call_target="tpu_custom_call" | custom-call | flops 8999999488 | bytes 21000000 | tf_op jit(solution)/shard_map/pallas_call | solution.py:621
  82.0 2.5 %shard_map.77 = (f32[3968,128]{1,0:T(8,128)}, f32[32,512]{1,0:T(8,128)}, f32[64,256]{1,0:T(8,128)}) custom-call(f32[3968,128]{1,0:T(8,128)} %get-tuple-element.9.upd_in, f32[32,512]{1,0:T(8,128)} %get-tuple-element.10.last_in, f32[64,256]{1,0:T(8,128)} %get-tuple-element.11.prev_in), custom_call_target="tpu_custom_call" | custom-call | tf_op jit(solution)/shard_map/pallas_call | solution.py:634

commit v3 on v2

--- a/solution.py
+++ b/solution.py
@@ -19,8 +19,8 @@
 GROUP = 6
 STEPS = 2 * ROUNDS
 AHEAD = 12
-LAG_ADD = 6
-LAG_END = 12
+LAG_ADD = 10
+LAG_END = 20
 SLOTS = LAG_END + 2
 PIECES = 4
 GROUPS = 5
@@ -182,7 +182,9 @@
 
             @functools.partial(each, 0, COLS // 2)
             def _(half):
-                other = 2 * half + odd
+                x = lax.rem(lax.div(j, 4) + lax.div(half, 2), 4)
+                y = lax.rem(lax.rem(j, 4) + 2 * lax.rem(half, 2), 4)
+                other = 4 * x + y + lax.rem(x + y + odd, 2) * (1 - 2 * lax.rem(y, 2))
 
                 @pl.when(other != j)
                 def _():
@@ -269,8 +271,8 @@
 
     out_last = pltpu.make_async_copy(sol_out.at[core], last_hbm, sem_out.at[0])
 
-    my_set = lax.rem(j, 2)
     my_chip = lax.div(j, 4)
+    my_set = lax.rem(j + my_chip, 2)
 
     def s_copy(other):
         spot = sol_t.at[my_set, my_chip]
@@ -437,11 +439,12 @@
             begin[spot] = turn[pl.ds(pl.multiple_of(core * OWN, OWN), OWN), :]
 
         full_both(t).wait_recv()
-        sides = sides_of(side)
+        half = lax.rem(side + z, 2)
+        sides = sides_of(half)
         terms = prod[n, rows_of(z), :] + full_in[n, 1].astype(F32) + full_in[n, 0].astype(F32)
         done = begin[spot, sides, :] - terms
         for part in range(2):
-            where = side * (WIDE * 2 * ROUNDS) + 2 * k + part
+            where = half * (WIDE * 2 * ROUNDS) + 2 * k + part
             upd[pl.ds(where, WIDE, stride=2 * ROUNDS), :] = done[:, part * 128 : part * 128 + 128]
 
         @pl.when(spot == 0)

time: 84.6 us -> 81 us (0.957)
  the two profiles are of different devices: /device:TPU:28 before, /device:TPU:0 now
where the time goes in v3:
time: 81 us; the launch traced here: 79.6 us
  Pallas kernels  79 us (98%)
    pallas_call x1, Pallas kernels, per_device(): pl.pallas_call(kernel, out_shape=out_shape, in_specs=[anywhere] * 5, out_...  76.5 us
    pallas_call x1, Pallas kernels, per_device(): pl.pallas_call(hand_over, out_shape=out_shape, in_specs=[anywhere] * 3, o...  2.5 us

profile of v3, /device:TPU:0, one launch (start us, length us, event | category | flops | bytes accessed | tf_op | source)
XLA Modules:
  0.0 79.6 jit_solution(1201829613714022712)
XLA Ops:
  0.6 76.5 %shard_map.76 = (f32[3968,128]{1,0:T(8,128)}, f32[32,512]{1,0:T(8,128)}, f32[64,256]{1,0:T(8,128)}) custom-call(bf16[31,512,256]{2,1,0:T(8,128)(2,1)} %bitcast.11, bf16[31,256,512]{2,1,0:T(8,128)(2,1)} %bitcast.12, f32[32,512]{1,0:T(8,128)} %bitcast.15, bf16[512,4096]{1,0:T(8,128)(2,1)} %inv_hbm.1, bf16[256,4096]{1,0:T(8,128)(2,1)} %bitcast.13), custom_call_target="tpu_custom_call" | custom-call | flops 8999999488 | bytes 21000000 | tf_op jit(solution)/shard_map/pallas_call | solution.py:624
  77.1 2.5 %shard_map.77 = (f32[3968,128]{1,0:T(8,128)}, f32[32,512]{1,0:T(8,128)}, f32[64,256]{1,0:T(8,128)}) custom-call(f32[3968,128]{1,0:T(8,128)} %get-tuple-element.9.upd_in, f32[32,512]{1,0:T(8,128)} %get-tuple-element.10.last_in, f32[64,256]{1,0:T(8,128)} %get-tuple-element.11.prev_in), custom_call_target="tpu_custom_call" | custom-call | tf_op jit(solution)/shard_map/pallas_call | solution.py:637

commit v4 on v3

--- a/solution.py
+++ b/solution.py
@@ -18,7 +18,7 @@
 OWN = 64
 GROUP = 6
 STEPS = 2 * ROUNDS
-AHEAD = 12
+AHEAD = 3
 LAG_ADD = 10
 LAG_END = 20
 SLOTS = LAG_END + 2
@@ -296,19 +296,20 @@
         own = lax.fori_loop(i + 1, ROWS, add_one, own)
         sol_t[my_set, my_chip] = own.astype(BF16)
 
-        @functools.partial(each, 1, COLS)
+        @functools.partial(each, 0, COLS)
         def _(d):
-            s_copy(lax.rem(j + d, COLS)).start()
+            x = lax.rem(my_chip + lax.rem(lax.div(d, 2), 4), 4)
+            y = 2 * lax.rem(1 + home + lax.div(d, 8), 2) + lax.rem(d, 2)
+            other = 4 * x + y
+
+            @pl.when(other != j)
+            def _():
+                s_copy(other).start()
 
         sol_out[0] = own[:, :SHARE]
         sol_out[1] = own[:, SHARE:]
         pair_copy().start()
 
-    @pl.when(core != home)
-    def _():
-        pair_in().wait_recv()
-
-    out_last.start()
 
     def solved(side):
         @functools.partial(each, 0, RING)
@@ -352,6 +353,11 @@
 
     def sides_of(side):
         return pl.ds(pl.multiple_of(side * WIDE, WIDE), WIDE)
+
+    def upd_copy(t):
+        sides = sides_of(lax.rem(side_of(t) + z, 2))
+        k = round_of(spot_of(t))
+        return pltpu.make_async_copy(upd.at[k, sides], upd_hbm.at[k, sides], sem_upd)
 
     def rows_of(chip):
         return pl.ds(pl.multiple_of(chip * WIDE, WIDE), WIDE)
@@ -432,24 +438,18 @@
         k = round_of(spot)
         n = lax.rem(t, SLOTS)
 
-        @pl.when(side == 0)
-        def _():
-            block = known[k, :, pl.ds(pl.multiple_of(z * 128, 128), 128)]
-            turn[...] = block.astype(F32).T
-            begin[spot] = turn[pl.ds(pl.multiple_of(core * OWN, OWN), OWN), :]
-
         full_both(t).wait_recv()
         half = lax.rem(side + z, 2)
         sides = sides_of(half)
         terms = prod[n, rows_of(z), :] + full_in[n, 1].astype(F32) + full_in[n, 0].astype(F32)
-        done = begin[spot, sides, :] - terms
-        for part in range(2):
-            where = half * (WIDE * 2 * ROUNDS) + 2 * k + part
-            upd[pl.ds(where, WIDE, stride=2 * ROUNDS), :] = done[:, part * 128 : part * 128 + 128]
+        done = begin[k, sides, :] - terms
+        upd[k, sides, :] = done
 
         @pl.when(spot == 0)
         def _():
             prior[sides, :] = done.astype(BF16)
+
+        upd_copy(t).start()
 
     def step(t):
         @pl.when(t < STEPS)
@@ -463,6 +463,12 @@
         @pl.when(t >= LAG_END)
         def _():
             third(t - LAG_END)
+
+    @functools.partial(each, 0, ROUNDS)
+    def _(k):
+        block = known[k, :, pl.ds(pl.multiple_of(z * 128, 128), 128)]
+        turn[...] = block.astype(F32).T
+        begin[k] = turn[pl.ds(pl.multiple_of(core * OWN, OWN), OWN), :]
 
     solved(0)
     each(0, AHEAD, step)
@@ -489,9 +495,6 @@
 
     each(AHEAD + LAG_END + 1, STEPS + LAG_END, step)
 
-    out_upd = pltpu.make_async_copy(upd, upd_hbm, sem_upd)
-    out_upd.start()
-
     def add_m(other, total):
         m_in(other).wait_recv()
         return total + recv_m[other].astype(F32)
@@ -499,6 +502,12 @@
     prev_out[...] = lax.fori_loop(j + 1, COLS, add_m, own_m[...])
     out_prev = pltpu.make_async_copy(prev_out, sol_prev_hbm, sem_out.at[1])
     out_prev.start()
+
+    @pl.when(core != home)
+    def _():
+        pair_in().wait_recv()
+
+    out_last.start()
 
     b_all(0).wait_send()
     b_all(1).wait_send()
@@ -531,27 +540,43 @@
         half_both(t).wait_send()
         full_both(t).wait_send()
 
-    out_upd.wait()
+    pltpu.make_async_copy(upd, upd_hbm, sem_upd).wait()
     out_last.wait()
     out_prev.wait()
 
 
-def hand_over(upd_in, last_in, prev_in, upd_out, last_out, prev_out, upd, last, prev, sems):
-    def piece(ref, n):
-        rows = ref.shape[0] // PIECES
-        return ref.at[pl.ds(n * rows, rows)]
-
-    moves = [(last_in, last, last_out), (prev_in, prev, prev_out)]
-    moves += [(piece(upd_in, n), piece(upd, n), piece(upd_out, n)) for n in range(PIECES)]
-    loads = [pltpu.make_async_copy(a, b, sems.at[0, n]) for n, (a, b, _) in enumerate(moves)]
-    stores = [pltpu.make_async_copy(b, c, sems.at[1, n]) for n, (_, b, c) in enumerate(moves)]
-    for load in loads:
-        load.start()
-    for load, store in zip(loads, stores):
-        load.wait()
-        store.start()
-    for store in stores:
-        store.wait()
+def hand_over(upd_in, last_in, prev_in, upd_out, last_out, prev_out, got, upd, last, prev, sems):
+    sides = OWN // PIECES
+    small = [(last_in, last, last_out), (prev_in, prev, prev_out)]
+
+    def load(n):
+        rows = pl.ds(n * sides, sides)
+        return pltpu.make_async_copy(upd_in.at[:, rows], got.at[:, rows], sems.at[0, n])
+
+    def store(n):
+        rows = pl.ds(n * sides * 2 * ROUNDS, sides * 2 * ROUNDS)
+        return pltpu.make_async_copy(upd.at[rows], upd_out.at[rows], sems.at[1, n])
+
+    loads = [load(n) for n in range(PIECES)]
+    stores = [store(n) for n in range(PIECES)]
+    for n, (start, middle, end) in enumerate(small):
+        loads.append(pltpu.make_async_copy(start, middle, sems.at[0, PIECES + n]))
+        stores.append(pltpu.make_async_copy(middle, end, sems.at[1, PIECES + n]))
+    for copy in loads:
+        copy.start()
+    for n, copy in enumerate(loads):
+        copy.wait()
+        if n < PIECES:
+            for k in range(ROUNDS):
+                block = got[k, n * sides : (n + 1) * sides, :]
+                for part in range(2):
+                    where = n * sides * 2 * ROUNDS + 2 * k + part
+                    upd[pl.ds(where, sides, stride=2 * ROUNDS), :] = block[
+                        :, part * 128 : part * 128 + 128
+                    ]
+        stores[n].start()
+    for copy in stores:
+        copy.wait()
 
 
 def scratch():
@@ -578,7 +603,7 @@
         pltpu.VMEM((SLOTS, 2, WIDE, BLOCK), BF16),
         pltpu.VMEM((128, BLOCK), F32),
         pltpu.VMEM((ROUNDS, OWN, BLOCK), F32),
-        pltpu.VMEM((OWN * ROUNDS * 2, 128), F32),
+        pltpu.VMEM((ROUNDS, OWN, BLOCK), F32),
         pltpu.VMEM((OWN, BLOCK), BF16),
         pltpu.VMEM((OWN, BLOCK), F32),
         pltpu.VMEM((COLS, OWN, BLOCK), BF16),
@@ -623,7 +648,7 @@
     ]
     results = pl.pallas_call(
         kernel,
-        out_shape=out_shape,
+        out_shape=[jax.ShapeDtypeStruct((ROUNDS, OWN, BLOCK), F32)] + out_shape[1:],
         in_specs=[anywhere] * 5,
         out_specs=[anywhere] * 3,
         scratch_shapes=scratch(),
@@ -639,7 +664,8 @@
         out_shape=out_shape,
         in_specs=[anywhere] * 3,
         out_specs=[anywhere] * 3,
-        scratch_shapes=[pltpu.VMEM(shape.shape, shape.dtype) for shape in out_shape]
+        scratch_shapes=[pltpu.VMEM((ROUNDS, OWN, BLOCK), F32)]
+        + [pltpu.VMEM(shape.shape, shape.dtype) for shape in out_shape]
         + [pltpu.SemaphoreType.DMA((2, PIECES + 2))],
         compiler_params=pltpu.CompilerParams(vmem_limit_bytes=60 * 1024 * 1024),
     )(*results)

time: 81 us -> 79.9 us (0.986); the launches traced: 79.6 us -> 79.8 us
  no operation moved by 1% of the time
where the time goes in v4:
time: 79.9 us; the launch traced here: 79.8 us
  Pallas kernels  79.1 us (99%)
    pallas_call x1, Pallas kernels, per_device(): pl.pallas_call(kernel, out_shape=[jax.ShapeDtypeStruct((ROUNDS, OWN, BLOC...  76.6 us
    pallas_call x1, Pallas kernels, per_device(): pl.pallas_call(hand_over, out_shape=out_shape, in_specs=[anywhere] * 3, o...  2.49 us

profile of v4, /device:TPU:0, one launch (start us, length us, event | category | flops | bytes accessed | tf_op | source)
XLA Modules:
  0.0 79.8 jit_solution(10465034577100038431)
XLA Ops:
  0.6 76.6 %shard_map.76 = (f32[31,64,256]{2,1,0:T(8,128)}, f32[32,512]{1,0:T(8,128)}, f32[64,256]{1,0:T(8,128)}) custom-call(bf16[31,512,256]{2,1,0:T(8,128)(2,1)} %bitcast.11, bf16[31,256,512]{2,1,0:T(8,128)(2,1)} %bitcast.12, f32[32,512]{1,0:T(8,128)} %bitcast.15, bf16[512,4096]{1,0:T(8,128)(2,1)} %inv_hbm.1, bf16[256,4096]{1,0:T(8,128)(2,1)} %bitcast.13), custom_call_target="tpu_custom_call" | custom-call | flops 8999999488 | bytes 21000000 | tf_op jit(solution)/shard_map/pallas_call | solution.py:649
  77.3 2.5 %shard_map.77 = (f32[3968,128]{1,0:T(8,128)}, f32[32,512]{1,0:T(8,128)}, f32[64,256]{1,0:T(8,128)}) custom-call(f32[31,64,256]{2,1,0:T(8,128)} %get-tuple-element.9.upd_in, f32[32,512]{1,0:T(8,128)} %get-tuple-element.10.last_in, f32[64,256]{1,0:T(8,128)} %get-tuple-element.11.prev_in), custom_call_target="tpu_custom_call" | custom-call | tf_op jit(solution)/shard_map/pallas_call | solution.py:662

commit v5 on v4

--- a/solution.py
+++ b/solution.py
@@ -245,7 +245,8 @@
         return remote(send_e.at[0], recv_e.at[other], e_send.at[0], e_recv.at[other], other, j)
 
     @functools.partial(each, 0, z + 1)
-    def _(chip):
+    def _(step):
+        chip = jnp.where((z == 3) & (step < 2), 1 - step, step)
         left = jnp.dot(forward_t, inv_block(2 * chip), preferred_element_type=F32)
         right = jnp.dot(forward_t, inv_block(2 * chip + 1), preferred_element_type=F32)
         mine = jnp.logical_and(chip == z, core == home)
@@ -321,24 +322,24 @@
     def half_copy(t, up):
         n = lax.rem(t, SLOTS)
         return remote(
-            half_out.at[n, up], half_in.at[n, up], half_send.at[n], half_recv.at[n],
+            half_out.at[t, up], half_in.at[n, up], half_send, half_recv.at[n],
             row_up if up else row_dn, j,
         )
 
     def half_both(t):
         n = lax.rem(t, SLOTS)
-        return remote(half_out.at[n], half_in.at[n], half_send.at[n], half_recv.at[n], row_up, j)
+        return remote(half_out.at[t], half_in.at[n], half_send, half_recv.at[n], row_up, j)
 
     def full_copy(t, up):
         n = lax.rem(t, SLOTS)
         return remote(
-            full_out.at[n, up], full_in.at[n, up], full_send.at[n], full_recv.at[n],
+            full_out.at[t, up], full_in.at[n, up], full_send, full_recv.at[n],
             row_up if up else row_dn, j,
         )
 
     def full_both(t):
         n = lax.rem(t, SLOTS)
-        return remote(full_out.at[n], full_in.at[n], full_send.at[n], full_recv.at[n], row_up, j)
+        return remote(full_out.at[t], full_in.at[n], full_send, full_recv.at[n], row_up, j)
 
     def side_of(t):
         late = lax.rem(lax.max(t - 2 * AHEAD, 0), 2)
@@ -406,13 +407,9 @@
             prod[n] = both[: RING * WIDE]
             prod[lax.rem(t + 1, SLOTS)] = both[RING * WIDE :]
 
-        @pl.when(t >= SLOTS)
-        def _():
-            half_both(t).wait_send()
-
         far = prod[n, rows_of(z_far), :].astype(BF16)
-        half_out[n, 1] = far[:16]
-        half_out[n, 0] = far[16:]
+        half_out[t, 1] = far[:16]
+        half_out[t, 0] = far[16:]
         half_copy(t, 1).start()
         half_copy(t, 0).start()
 
@@ -420,17 +417,13 @@
         n = lax.rem(t, SLOTS)
         half_both(t).wait_recv()
 
-        @pl.when(t >= SLOTS)
-        def _():
-            full_both(t).wait_send()
-
         up = prod[n, rows_of(z_up), :]
-        full_out[n, 1, 0:16] = (up[0:16] + half_in[n, 1].astype(F32)).astype(BF16)
-        full_out[n, 1, 16:32] = up[16:32].astype(BF16)
+        full_out[t, 1, 0:16] = (up[0:16] + half_in[n, 1].astype(F32)).astype(BF16)
+        full_out[t, 1, 16:32] = up[16:32].astype(BF16)
         full_copy(t, 1).start()
         dn = prod[n, rows_of(z_dn), :]
-        full_out[n, 0, 0:16] = dn[0:16].astype(BF16)
-        full_out[n, 0, 16:32] = (dn[16:32] + half_in[n, 0].astype(F32)).astype(BF16)
+        full_out[t, 0, 0:16] = dn[0:16].astype(BF16)
+        full_out[t, 0, 16:32] = (dn[16:32] + half_in[n, 0].astype(F32)).astype(BF16)
         full_copy(t, 0).start()
 
     def third(t):
@@ -535,10 +528,8 @@
     def _(b):
         m_copy(b).wait_send()
 
-    @functools.partial(each, STEPS - SLOTS, STEPS)
-    def _(t):
-        half_both(t).wait_send()
-        full_both(t).wait_send()
+    remote(half_out, half_out, half_send, half_recv.at[0], row_up, j).wait_send()
+    remote(full_out, full_out, full_send, full_recv.at[0], row_up, j).wait_send()
 
     pltpu.make_async_copy(upd, upd_hbm, sem_upd).wait()
     out_last.wait()
@@ -597,9 +588,9 @@
         pltpu.VMEM((2, WIDE, SHARE), F32),
         pltpu.VMEM((2, RING, WIDE, 2 * SHARE), BF16),
         pltpu.VMEM((SLOTS, RING * WIDE, BLOCK), F32),
+        pltpu.VMEM((STEPS, 2, WIDE // 2, BLOCK), BF16),
         pltpu.VMEM((SLOTS, 2, WIDE // 2, BLOCK), BF16),
-        pltpu.VMEM((SLOTS, 2, WIDE // 2, BLOCK), BF16),
-        pltpu.VMEM((SLOTS, 2, WIDE, BLOCK), BF16),
+        pltpu.VMEM((STEPS, 2, WIDE, BLOCK), BF16),
         pltpu.VMEM((SLOTS, 2, WIDE, BLOCK), BF16),
         pltpu.VMEM((128, BLOCK), F32),
         pltpu.VMEM((ROUNDS, OWN, BLOCK), F32),
@@ -627,9 +618,9 @@
         dma(()),
         dma(()),
         dma((2, RING)),
+        dma(()),
         dma((SLOTS,)),
-        dma((SLOTS,)),
-        dma((SLOTS,)),
+        dma(()),
         dma((SLOTS,)),
         dma((COLS,)),
         dma((COLS,)),

time: 79.9 us -> 79.5 us (level)
  no operation moved by 1% of the time
where the time goes in v5:
time: 79.5 us; the launch traced here: 79.4 us
  Pallas kernels  78.7 us (99%)
    pallas_call x1, Pallas kernels, per_device(): pl.pallas_call(kernel, out_shape=[jax.ShapeDtypeStruct((ROUNDS, OWN, BLOC...  76.2 us
    pallas_call x1, Pallas kernels, per_device(): pl.pallas_call(hand_over, out_shape=out_shape, in_specs=[anywhere] * 3, o...  2.49 us

profile of v5, /device:TPU:0, one launch (start us, length us, event | category | flops | bytes accessed | tf_op | source)
XLA Modules:
  0.0 79.4 jit_solution(15870809515059827686)
XLA Ops:
  0.6 76.2 %shard_map.76 = (f32[31,64,256]{2,1,0:T(8,128)}, f32[32,512]{1,0:T(8,128)}, f32[64,256]{1,0:T(8,128)}) custom-call(bf16[31,512,256]{2,1,0:T(8,128)(2,1)} %bitcast.11, bf16[31,256,512]{2,1,0:T(8,128)(2,1)} %bitcast.12, f32[32,512]{1,0:T(8,128)} %bitcast.15, bf16[512,4096]{1,0:T(8,128)(2,1)} %inv_hbm.1, bf16[256,4096]{1,0:T(8,128)(2,1)} %bitcast.13), custom_call_target="tpu_custom_call" | custom-call | flops 8999999488 | bytes 21000000 | tf_op jit(solution)/shard_map/pallas_call | solution.py:640
  76.9 2.5 %shard_map.77 = (f32[3968,128]{1,0:T(8,128)}, f32[32,512]{1,0:T(8,128)}, f32[64,256]{1,0:T(8,128)}) custom-call(f32[31,64,256]{2,1,0:T(8,128)} %get-tuple-element.9.upd_in, f32[32,512]{1,0:T(8,128)} %get-tuple-element.10.last_in, f32[64,256]{1,0:T(8,128)} %get-tuple-element.11.prev_in), custom_call_target="tpu_custom_call" | custom-call | tf_op jit(solution)/shard_map/pallas_call | solution.py:653

commit v6 on v5

--- a/solution.py
+++ b/solution.py
@@ -655,8 +655,12 @@
         out_shape=out_shape,
         in_specs=[anywhere] * 3,
         out_specs=[anywhere] * 3,
-        scratch_shapes=[pltpu.VMEM((ROUNDS, OWN, BLOCK), F32)]
-        + [pltpu.VMEM(shape.shape, shape.dtype) for shape in out_shape]
+        scratch_shapes=[
+            pltpu.VMEM((ROUNDS, OWN, BLOCK), F32),
+            pltpu.VMEM((OWN * ROUNDS * 2 + 64, 128), F32),
+            pltpu.VMEM((WIDE, SHARE), F32),
+            pltpu.VMEM((OWN, BLOCK), F32),
+        ]
         + [pltpu.SemaphoreType.DMA((2, PIECES + 2))],
         compiler_params=pltpu.CompilerParams(vmem_limit_bytes=60 * 1024 * 1024),
     )(*results)

time: 79.5 us -> 79.5 us (level)
  no operation moved by 1% of the time
where the time goes in v6:
time: 79.5 us; the launch traced here: 79.4 us
  Pallas kernels  78.7 us (99%)
    pallas_call x1, Pallas kernels, per_device(): pl.pallas_call(kernel, out_shape=[jax.ShapeDtypeStruct((ROUNDS, OWN, BLOC...  76.2 us
    pallas_call x1, Pallas kernels, per_device(): pl.pallas_call(hand_over, out_shape=out_shape, in_specs=[anywhere] * 3, o...  2.49 us

profile of v6, /device:TPU:0, one launch (start us, length us, event | category | flops | bytes accessed | tf_op | source)
XLA Modules:
  0.0 79.4 jit_solution(3039332852571723184)
XLA Ops:
  0.6 76.2 %shard_map.76 = (f32[31,64,256]{2,1,0:T(8,128)}, f32[32,512]{1,0:T(8,128)}, f32[64,256]{1,0:T(8,128)}) custom-call(bf16[31,512,256]{2,1,0:T(8,128)(2,1)} %bitcast.11, bf16[31,256,512]{2,1,0:T(8,128)(2,1)} %bitcast.12, f32[32,512]{1,0:T(8,128)} %bitcast.15, bf16[512,4096]{1,0:T(8,128)(2,1)} %inv_hbm.1, bf16[256,4096]{1,0:T(8,128)(2,1)} %bitcast.13), custom_call_target="tpu_custom_call" | custom-call | flops 8999999488 | bytes 21000000 | tf_op jit(solution)/shard_map/pallas_call | solution.py:640
  76.9 2.5 %shard_map.77 = (f32[3968,128]{1,0:T(8,128)}, f32[32,512]{1,0:T(8,128)}, f32[64,256]{1,0:T(8,128)}) custom-call(f32[31,64,256]{2,1,0:T(8,128)} %get-tuple-element.9.upd_in, f32[32,512]{1,0:T(8,128)} %get-tuple-element.10.last_in, f32[64,256]{1,0:T(8,128)} %get-tuple-element.11.prev_in), custom_call_target="tpu_custom_call" | custom-call | tf_op jit(solution)/shard_map/pallas_call | solution.py:653
